TPU v7x, 32 devices: a whole 2x2x4 slice. The times are simulated.
32 devices in a mesh: groups: 2 (over y), pool: 8 (over z, x), tp: 2 (over core).
Axes of the slice: x: 2, y: 2, z: 4, core: 2. Of those that a mesh axis runs over, the one named last changes fastest.
Arguments:
- prompt_states: bfloat16 [1024, 7168], P(('groups', 'pool'), 'tp'), parts along dimension 0, may hold values from -6 to 6
- down_kv: bfloat16 [7168, 576], P('tp'), may hold values from -0.0625 to 0.0625
- kv_gain: float32 [512], replicated, may hold values from 0.1 to 1.9
- queries: bfloat16 [64, 128, 576], P(('groups', 'pool'), 'tp'), parts along dimension 0, may hold values from -110 to 110
- row_prompt: int32 [64], P(('groups', 'pool')), parts along dimension 0, may hold values from 0 to 3, as said below
- prompt_len: int32 [8], P('groups'), parts along dimension 0, may hold values from 1 to 128, as said below
Outputs:
- attended: bfloat16 [64, 128, 512], P(('groups', 'pool'), 'tp'), parts along dimension 0
There are 2 independent parts, one for each index of `groups`. A program takes and returns all parts, laid end to end along the dimension named above; an argument that names none is the same for every part. Nothing has to cross between parts.
Inputs may be any that keep to these rules, and one draw needn't show every extreme that they name: `row_prompt`: the rows fall in 4 aligned blocks of 8 rows; every row of block b continues prompt b XOR s, with one s of 0 to 3 for the whole draw. `prompt_len`: some prompt has all 128 tokens.
All inputs are finite; a program needn't handle non-finite values.
Results may differ from a plain program's by a relative error of at most 0.0045.
The roundings to bfloat16 on the way count: a program that leaves them out, or rounds other values in their place, can miss the bound.
Values may be sent and summed in bfloat16 or wider, within the bound.
No kernel may reach another device: no remote copies, remote signals or barrier semaphores. Data moves between devices by JAX's collectives and lax.ppermute only.
A program may use at most 64 MiB of HBM per device.

v0:
```python
import functools

import jax
import jax.numpy as jnp
from jax import lax
from jax.experimental import pallas as pl
from jax.experimental.pallas import tpu as pltpu
from jax.sharding import PartitionSpec as P

score_scale = 192.0 ** (-0.5)
masked_score = -1e30
lanes = 128
VMEM = pltpu.VMEM
whole_vmem = pl.BlockSpec(memory_space=pltpu.VMEM)
whole_smem = pl.BlockSpec(memory_space=pltpu.SMEM)
in_hbm = pl.BlockSpec(memory_space=pltpu.HBM)


def last_dims_dot(left, right):
    return lax.dot_general(left, right, (((1,), (1,)), ((), ())), preferred_element_type=jnp.float32)


def project_kernel(chunk, states_hbm, weights_hbm, partial_ref, states, weights, states_sem, sems):
    depth = states_hbm.shape[1]
    states_copy = pltpu.make_async_copy(states_hbm, states, states_sem)
    states_copy.start()
    copies = []
    for index in range(depth // chunk):
        columns = pl.ds(index * chunk, chunk)
        copy = pltpu.make_async_copy(weights_hbm.at[:, columns], weights.at[:, columns], sems.at[index])
        copy.start(priority=1)
        copies.append(copy)
    states_copy.wait()
    total = None
    for index, copy in enumerate(copies):
        copy.wait()
        columns = pl.ds(index * chunk, chunk)
        part = last_dims_dot(states[:, columns], weights[:, columns])
        total = part if total is None else total + part
    partial_ref[...] = total


def angle_kernel(seq_len, cosine_ref, sine_ref):
    tokens, width = cosine_ref.shape
    half = width // 2
    first = lax.rem(lax.axis_index("pool") * tokens, seq_len)
    position = (first + lax.broadcasted_iota(jnp.int32, (tokens, width), 0)).astype(jnp.float32)
    column = lax.broadcasted_iota(jnp.int32, (tokens, width), 1)
    front = column < half
    index = jnp.where(front, column, column - half).astype(jnp.float32)
    angles = position * jnp.exp(index * (-2.0 / width * 9.210340371976184))
    cosine_ref[...] = jnp.cos(angles)
    sine = jnp.sin(angles)
    sine_ref[...] = jnp.where(front, -sine, sine)


def mask_kernel(axes, owner_hbm, lengths_hbm, query_hbm, bias_ref, query_ref, owner, lengths, sems):
    small = [
        pltpu.make_async_copy(owner_hbm, owner, sems.at[0]),
        pltpu.make_async_copy(lengths_hbm, lengths, sems.at[1]),
    ]
    fetch = pltpu.make_async_copy(query_hbm, query_ref, sems.at[2])
    for copy in [*small, fetch]:
        copy.start()
    seq_len = bias_ref.shape[1]
    slot = lax.broadcasted_iota(jnp.int32, bias_ref.shape, 1)
    if axes:
        slot = slot + lax.rem(sum(lax.axis_index(axis) for axis in axes), 2) * (seq_len // 2)
        slot = jnp.where(slot >= seq_len, slot - seq_len, slot)
    for copy in small:
        copy.wait()
    bias_ref[...] = jnp.where(slot < lengths[owner[0]], 0.0, masked_score)
    fetch.wait()


def encode_kernel(packed, mine_ref, other_ref, gain_ref, cosine_ref, sine_ref, cache_ref):
    rank = gain_ref.shape[1]
    tokens, width = cosine_ref.shape
    projected = mine_ref[...] + other_ref[...]
    content = projected[:, :rank]
    mean = jnp.mean(content * content, axis=1, keepdims=True)
    normed = (content * lax.rsqrt(mean + 1e-06) * gain_ref[...]).astype(cache_ref.dtype)
    rotary = projected[:, rank:]
    swapped = jnp.concatenate([rotary[:, width // 2 :], rotary[:, : width // 2]], axis=1)
    rotated = rotary * cosine_ref[...] + swapped * sine_ref[...]
    if packed:
        for index in range(rank // lanes):
            cache_ref[index * tokens : (index + 1) * tokens, :] = normed[:, index * lanes : (index + 1) * lanes]
        paired_rows = jnp.concatenate([rotated[: tokens // 2], rotated[tokens // 2 :]], axis=1)
        cache_ref[rank // lanes * tokens :, :] = paired_rows.astype(cache_ref.dtype)
    else:
        cache_ref[:, :rank] = normed
        cache_ref[:, rank:] = rotated.astype(cache_ref.dtype)


def attend_kernel(packed, query_ref, bias_ref, *refs):
    count = 2 if packed else 1
    blocks, out_hbm, out, keys, sems = refs[:count], *refs[count:]
    rows, heads, rank = out_hbm.shape
    if packed:
        tokens = keys.shape[0] // 2
        width = keys.shape[1] - rank
        for half, block in enumerate(blocks):
            first = half * tokens
            for index in range(rank // lanes):
                keys[first : first + tokens, index * lanes : (index + 1) * lanes] = block[
                    index * tokens : (index + 1) * tokens, :
                ]
            paired_rows = block[rank // lanes * tokens :, :]
            keys[first : first + tokens // 2, rank:] = paired_rows[:, :width]
            keys[first + tokens // 2 : first + tokens, rank:] = paired_rows[:, width:]
    else:
        keys = blocks[0]
    query = query_ref[...].reshape(rows * heads, query_ref.shape[2])
    parts = sems.shape[0]
    per = rows // parts
    spans = [slice(part * per * heads, (part + 1) * per * heads) for part in range(parts)]
    products = [last_dims_dot(query[span], keys[...]) for span in spans]
    rounded, inverse = [], []
    for product in products:
        score = product * score_scale + bias_ref[...]
        weights = jnp.exp(score - jnp.max(score, axis=1, keepdims=True))
        inverse.append(1.0 / jnp.sum(weights, axis=1, keepdims=True))
        rounded.append(weights.astype(jnp.bfloat16))
    sums = [jnp.dot(part, keys[:, :rank], preferred_element_type=jnp.float32) for part in rounded]
    copies = []
    for part in range(parts):
        mine = pl.ds(part * per, per)
        out[mine] = (sums[part] * inverse[part]).astype(out.dtype).reshape(per, heads, rank)
        copy = pltpu.make_async_copy(out.at[mine], out_hbm.at[mine], sems.at[part])
        copy.start()
        copies.append(copy)
    for copy in copies:
        copy.wait()


def per_device(prompt_states, down_kv, kv_gain, queries, row_prompt, prompt_len):
    tokens, depth = prompt_states.shape
    latent = down_kv.shape[1]
    rank = kv_gain.shape[0]
    half = (latent - rank) // 2
    prompts = prompt_len.shape[0]
    pool = lax.axis_size("pool")
    seq_len = tokens * pool // prompts
    block = pool // prompts
    pool_at = lax.axis_index("pool")
    shift = row_prompt[0] ^ (pool_at // block)
    packed = block == 2 and lax.axis_size("tp") == 2 and rank % lanes == 0 and 4 * half == lanes and tokens % 32 == 0
    cache_shape = (tokens * latent // lanes, lanes) if packed else (tokens, latent)

    chunk = 512 if depth % 512 == 0 else depth
    hbm = functools.partial(pltpu.with_memory_space_constraint, memory_space=pltpu.HBM)
    partial = pl.pallas_call(
        functools.partial(project_kernel, chunk),
        out_shape=jax.ShapeDtypeStruct((tokens, latent), jnp.float32),
        in_specs=[in_hbm, in_hbm],
        out_specs=whole_vmem,
        scratch_shapes=[
            VMEM((tokens, depth), jnp.bfloat16),
            VMEM((latent, depth), jnp.bfloat16),
            pltpu.SemaphoreType.DMA,
            pltpu.SemaphoreType.DMA((depth // chunk,)),
        ],
        compiler_params=pltpu.CompilerParams(vmem_limit_bytes=16 * 2**20),
        cost_estimate=pl.CostEstimate(flops=2 * tokens * depth * latent, bytes_accessed=2 * depth * (latent + tokens), transcendentals=0),
        name="project",
    )(hbm(prompt_states), hbm(down_kv.T))
    cosine, sine = pl.pallas_call(
        functools.partial(angle_kernel, seq_len),
        out_shape=[jax.ShapeDtypeStruct((tokens, 2 * half), jnp.float32)] * 2,
        out_specs=[whole_vmem] * 2,
        compiler_params=pltpu.CompilerParams(vmem_limit_bytes=4 * 2**20),
        cost_estimate=pl.CostEstimate(flops=100 * tokens * half, bytes_accessed=4096, transcendentals=4 * tokens * half),
        name="angles",
    )()

    other = lax.ppermute(partial, "tp", [(0, 1), (1, 0)])
    cache = pl.pallas_call(
        functools.partial(encode_kernel, packed),
        out_shape=jax.ShapeDtypeStruct(cache_shape, jnp.bfloat16),
        in_specs=[whole_vmem] * 5,
        out_specs=whole_vmem,
        compiler_params=pltpu.CompilerParams(vmem_limit_bytes=4 * 2**20),
        name="encode",
    )(partial, other, kv_gain[None, :], cosine, sine)

    def mask(*axes):
        return pl.pallas_call(
            functools.partial(mask_kernel, axes),
            out_shape=[
                jax.ShapeDtypeStruct((1, seq_len), jnp.float32),
                pltpu.VMEM(queries.shape, queries.dtype),
            ],
            in_specs=[in_hbm] * 3,
            out_specs=[whole_vmem] * 2,
            scratch_shapes=[
                pltpu.SMEM(row_prompt.shape, jnp.int32),
                pltpu.SMEM(prompt_len.shape, jnp.int32),
                pltpu.SemaphoreType.DMA((3,)),
            ],
            compiler_params=pltpu.CompilerParams(vmem_limit_bytes=4 * 2**20),
            cost_estimate=pl.CostEstimate(flops=1000, bytes_accessed=4096, transcendentals=0),
            name="mask_and_queries",
        )(hbm(row_prompt), hbm(prompt_len), hbm(queries))

    def attend(ready, *blocks):
        bias, fetched = ready
        parts = 2 if queries.shape[0] % 2 == 0 else 1
        return pl.pallas_call(
            functools.partial(attend_kernel, len(blocks) > 1),
            out_shape=pltpu.HBM((queries.shape[0], queries.shape[1], rank), jnp.bfloat16),
            in_specs=[whole_vmem] * (2 + len(blocks)),
            out_specs=in_hbm,
            scratch_shapes=[
                VMEM((queries.shape[0], queries.shape[1], rank), jnp.bfloat16),
                VMEM((seq_len if len(blocks) > 1 else 16, latent), jnp.bfloat16),
                pltpu.SemaphoreType.DMA((parts,)),
            ],
            compiler_params=pltpu.CompilerParams(vmem_limit_bytes=(32 if seq_len > 1024 else 8) * 2**20),
            name="attend",
        )(fetched, bias, *blocks)

    def paired_step(step):
        pairs = [
            (at * 2 + c, ((at // 2 ^ step) * 2 + (at % 2 ^ c)) * 2 + c) for at in range(pool) for c in range(2)
        ]

        def run(rows):
            if step == 0:
                there = lax.ppermute(rows, "pool", [(at, at ^ 1) for at in range(pool)])
                return attend(mask("pool"), rows, there)
            here = lax.ppermute(rows, ("pool", "tp"), pairs)
            here, bias = lax.optimization_barrier((here, mask("pool", "tp")))
            return attend(bias, here, lax.ppermute(here, "tp", [(0, 1), (1, 0)]))

        return run

    if packed:
        return lax.switch(shift, [paired_step(step) for step in range(prompts)], cache)

    def fetch(step):
        pairs = [(at, at ^ (step * block)) for at in range(pool)]
        return lambda rows: lax.ppermute(rows, "pool", pairs) if step else rows

    here = lax.switch(shift, [fetch(step) for step in range(prompts)], cache)
    members = [list(range(b * block, (b + 1) * block)) for b in range(prompts)]
    return attend(mask(), lax.all_gather(here, "pool", axis=0, tiled=True, axis_index_groups=members))


def solution(mesh):
    placed = (
        P(("groups", "pool"), "tp"),
        P("tp", None),
        P(),
        P(("groups", "pool"), "tp", None),
        P(("groups", "pool")),
        P("groups"),
    )
    return jax.shard_map(
        per_device,
        mesh=mesh,
        in_specs=placed,
        out_specs=P(("groups", "pool"), "tp", None),
        check_vma=False,
    )
```

profile of v0, /device:TPU:0, one launch (start us, length us, event | category | flops | bytes accessed | tf_op | source)
XLA Modules:
  0.0 14.1 jit_solution(4210833229410612933)
XLA Ops:
  0.0 0.0 copy-start
  0.0 3.0 %project.1.mine_ref = f32[64,576]{1,0:T(8,128)S(1)} custom-call(bf16[64,3584]{1,0:T(8,128)(2,1)} %states_hbm.1, bf16[576,3584]{1,0:T(8,128)(2,1)} %bitcast.5), custom_call_target="tpu_custom_call" | custom-call | flops 264241152 | bytes 4587520 | tf_op jit(solution)/shard_map/project/pallas_call | solution.py:153
  3.1 0.5 %collective-permute-start.7 = (f32[64,576]{1,0:T(8,128)S(1)}, f32[64,576]{1,0:T(8,128)S(1)}, u32[]{:S(2)}, u32[]{:S(2)}) collective-permute-start(f32[64,576]{1,0:T(8,128)S(1)} %project.1.mine_ref), channel_id=1, source_target_pairs={{0,1},{1,0},{2,3},{3,2},{4,5},{5,4},{6,7},{7,6},{8,9},{9,8},{10,11... | collective-permute-start | bytes 442376 | tf_op jit(solution)/shard_map/ppermute | solution.py:177
  3.6 0.1 %angles.1 = (f32[64,64]{1,0:T(8,128)S(1)}, f32[64,64]{1,0:T(8,128)S(1)}) custom-call(), custom_call_target="tpu_custom_call" | custom-call | flops 204800 | bytes 4096 | tf_op jit(solution)/shard_map/angles/pallas_call | solution.py:168
  4.4 0.2 %collective-permute-done.7.other_ref = f32[64,576]{1,0:T(8,128)S(1)} collective-permute-done((f32[64,576]{1,0:T(8,128)S(1)}, f32[64,576]{1,0:T(8,128)S(1)}, u32[]{:S(2)}, u32[]{:S(2)}) %collective-permute-start.7) | collective-permute-done | bytes 147488 | tf_op jit(solution)/shard_map/ppermute | solution.py:177
  4.6 0.0 copy-done
  4.6 0.1 %encode.1 = bf16[288,128]{1,0:T(8,128)(2,1)S(1)} custom-call(f32[64,576]{1,0:T(8,128)S(1)} %project.1.mine_ref, f32[64,576]{1,0:T(8,128)S(1)} %collective-permute-done.7.other_ref, f32[1,512]{1,0:T(1,128)S(1)} %bitcast.4, f32[64,64]{1,0:T(8,128)S(1)} %get-tuple-element.77.cosine_ref, f32[64,64]{1,0:T(8,128)S(1)} %get-tuple-element.78.sine_ref), custom_call_target="tpu_custom_call" | custom-call | tf_op jit(solution)/shard_map/encode/pallas_call | solution.py:178
  4.8 9.3 %conditional.1 = (bf16[4,64,512]{2,1,0:T(8,128)(2,1)}) conditional(s32[]{:T(128)} %clamp.3, (s32[4]{0:T(128)}, s32[4]{0:T(128)}, bf16[4,64,576]{2,1,0:T(8,128)(2,1)}, bf16[288,128]{1,0:T(8,128)(2,1)S(1)}) %tuple.20, (bf16[288,128]{1,0:T(8,128)(2,1)S(1)}, s32[4]{0:T(128)}, s32[4]{0:T(128)}, ...), branch_computations={%region_0.1_spmd, %region_1.2_spmd, %region_2.3_spmd, %region_3.4_... | conditional | flops 1000 | bytes 594008 | solution.py:239
  4.8 4.0 %collective-permute-start.3 = (bf16[288,128]{1,0:T(8,128)(2,1)S(1)}, bf16[288,128]{1,0:T(8,128)(2,1)S(1)}, u32[]{:S(2)}, u32[]{:S(2)}) collective-permute-start(bf16[288,128]{1,0:T(8,128)(2,1)S(1)} %get-tuple-element.57), channel_id=1, source_target_pairs={{0,8},{1,11},{2,10},{3,9},{4,12},{5,15},{6,14},{7,13},{8,0},{9,3},... | collective-permute-start | bytes 221192 | tf_op jit(solution)/shard_map/cond/branch_2_fun/ppermute | solution.py:232
  8.8 1.0 %mask_and_queries.6 = (f32[1,128]{1,0:T(1,128)S(1)}, bf16[4,64,576]{2,1,0:T(8,128)(2,1)S(1)}) custom-call(s32[4]{0:T(128)} %get-tuple-element.58.owner_hbm, s32[4]{0:T(128)} %get-tuple-element.59.lengths_hbm, bf16[4,64,576]{2,1,0:T(8,128)(2,1)} %get-tuple-element.60.query_hbm), custom_call_target="tpu_custom_call" | custom-call | flops 1000 | bytes 4096 | tf_op jit(solution)/shard_map/cond/branch_2_fun/mask_and_queries/pallas_call | solution.py:188
  9.8 1.8 %collective-permute-done.3.refs_0_ = bf16[288,128]{1,0:T(8,128)(2,1)S(1)} collective-permute-done((bf16[288,128]{1,0:T(8,128)(2,1)S(1)}, bf16[288,128]{1,0:T(8,128)(2,1)S(1)}, u32[]{:S(2)}, u32[]{:S(2)}) %collective-permute-start.3) | collective-permute-done | bytes 73760 | tf_op jit(solution)/shard_map/cond/branch_2_fun/ppermute | solution.py:232
  11.6 0.1 collective-permute-start.4
  11.6 1.2 %collective-permute-done.4.refs_1_ = bf16[288,128]{1,0:T(8,128)(2,1)S(1)} collective-permute-done((bf16[288,128]{1,0:T(8,128)(2,1)S(1)}, bf16[288,128]{1,0:T(8,128)(2,1)S(1)}, u32[]{:S(2)}, u32[]{:S(2)}) %collective-permute-start.4) | collective-permute-done | bytes 73760 | tf_op jit(solution)/shard_map/cond/branch_2_fun/ppermute | solution.py:234
  12.8 1.2 %attend.6 = bf16[4,64,512]{2,1,0:T(8,128)(2,1)} custom-call(bf16[4,64,576]{2,1,0:T(8,128)(2,1)S(1)} %get-tuple-element.63.query_ref, f32[1,128]{1,0:T(1,128)S(1)} %get-tuple-element.64.bias_ref, bf16[288,128]{1,0:T(8,128)(2,1)S(1)} %collective-permute-done.3.refs_0_, bf16[288,128]{1,0:T(8,128)(2,1)S(1)} %collective-permute-done.4.refs_1_), custom_call_target="tpu_custom_call" | custom-call | tf_op jit(solution)/shard_map/cond/branch_2_fun/attend/pallas_call | solution.py:209
Async XLA Ops:
  0.0 4.6 %copy-start = (f32[512]{0:T(512)S(1)}, f32[512]{0:T(512)}, u32[]{:S(2)}) copy-start(f32[512]{0:T(512)} %param.12) | copy-start | bytes 6148
  3.1 1.5 %collective-permute-start.7 = (f32[64,576]{1,0:T(8,128)S(1)}, f32[64,576]{1,0:T(8,128)S(1)}, u32[]{:S(2)}, u32[]{:S(2)}) collective-permute-start(f32[64,576]{1,0:T(8,128)S(1)} %project.1.mine_ref), channel_id=1, source_target_pairs={{0,1},{1,0},{2,3},{3,2},{4,5},{5,4},{6,7},{7,6},{8,9},{9,8},{10,11... | collective-permute-start | bytes 442376 | tf_op jit(solution)/shard_map/ppermute | solution.py:177
  4.8 6.8 %collective-permute-start.3 = (bf16[288,128]{1,0:T(8,128)(2,1)S(1)}, bf16[288,128]{1,0:T(8,128)(2,1)S(1)}, u32[]{:S(2)}, u32[]{:S(2)}) collective-permute-start(bf16[288,128]{1,0:T(8,128)(2,1)S(1)} %get-tuple-element.57), channel_id=1, source_target_pairs={{0,8},{1,11},{2,10},{3,9},{4,12},{5,15},{6,14},{7,13},{8,0},{9,3},... | collective-permute-start | bytes 221192 | tf_op jit(solution)/shard_map/cond/branch_2_fun/ppermute | solution.py:232
  11.6 1.3 %collective-permute-start.4 = (bf16[288,128]{1,0:T(8,128)(2,1)S(1)}, bf16[288,128]{1,0:T(8,128)(2,1)S(1)}, u32[]{:S(2)}, u32[]{:S(2)}) collective-permute-start(bf16[288,128]{1,0:T(8,128)(2,1)S(1)} %collective-permute-done.3.refs_0_), channel_id=1, source_target_pairs={{0,1},{1,0},{2,3},{3,2},{4,5},{5,4},{6,7},{7,6},{8,9},{9,8},{10,11... | collective-permute-start | bytes 221192 | tf_op jit(solution)/shard_map/cond/branch_2_fun/ppermute | solution.py:234
where the time goes:
time: 14 us; the launch traced here: 14.1 us
  Pallas kernels  5.56 us (40%)
  starting transfers between devices  4.61 us (33%)
  waiting for transfers between devices  3.16 us (23%)
  between operations  0.68 us (5%)
    ppermute x1, starting transfers between devices, run(): here = lax.ppermute(rows, ('pool', 'tp'), pairs)  4.01 us
    pallas_call x1, Pallas kernels, per_device(): pl.pallas_call(functools.partial(project_kernel, chunk), out_shape=jax.Sh...  3.05 us
    ppermute x1, waiting for transfers between devices, run(): here = lax.ppermute(rows, ('pool', 'tp'), pairs)  1.76 us
    pallas_call x1, Pallas kernels, attend(): pl.pallas_call(functools.partial(attend_kernel, len(blocks) > 1), out_sha...  1.22 us
    ppermute x1, waiting for transfers between devices, run(): return attend(bias, here, lax.ppermute(here, 'tp', [(0, 1), (1, 0)]))  1.19 us
    pallas_call x1, Pallas kernels, mask(): pl.pallas_call(functools.partial(mask_kernel, axes), out_shape=[jax.Shape...  1 us
    ppermute x1, starting transfers between devices, per_device(): other = lax.ppermute(partial, 'tp', [(0, 1), (1, 0)])  0.52 us
  transfers between devices with their start and end apart: 3, of which 3 were waited for; matrix products, arithmetic and copies ran while one was open for 0% of the time, Pallas kernels for 8%

commit v1 on v0

--- a/solution.py
+++ b/solution.py
@@ -20,21 +20,20 @@
     return lax.dot_general(left, right, (((1,), (1,)), ((), ())), preferred_element_type=jnp.float32)
 
 
-def project_kernel(chunk, states_hbm, weights_hbm, partial_ref, states, weights, states_sem, sems):
-    depth = states_hbm.shape[1]
+def project_kernel(spans, states_hbm, weights_hbm, partial_ref, states, weights, states_sem, sems):
     states_copy = pltpu.make_async_copy(states_hbm, states, states_sem)
     states_copy.start()
     copies = []
-    for index in range(depth // chunk):
-        columns = pl.ds(index * chunk, chunk)
+    for index, (first, width) in enumerate(spans):
+        columns = pl.ds(first, width)
         copy = pltpu.make_async_copy(weights_hbm.at[:, columns], weights.at[:, columns], sems.at[index])
         copy.start(priority=1)
         copies.append(copy)
     states_copy.wait()
     total = None
-    for index, copy in enumerate(copies):
+    for (first, width), copy in zip(spans, copies):
         copy.wait()
-        columns = pl.ds(index * chunk, chunk)
+        columns = pl.ds(first, width)
         part = last_dims_dot(states[:, columns], weights[:, columns])
         total = part if total is None else total + part
     partial_ref[...] = total
@@ -149,9 +148,11 @@
     cache_shape = (tokens * latent // lanes, lanes) if packed else (tokens, latent)
 
     chunk = 512 if depth % 512 == 0 else depth
+    edges = [0, *range(chunk // 2, depth, chunk), depth] if chunk < depth else [0, depth]
+    spans = [(start, end - start) for start, end in zip(edges, edges[1:])]
     hbm = functools.partial(pltpu.with_memory_space_constraint, memory_space=pltpu.HBM)
     partial = pl.pallas_call(
-        functools.partial(project_kernel, chunk),
+        functools.partial(project_kernel, spans),
         out_shape=jax.ShapeDtypeStruct((tokens, latent), jnp.float32),
         in_specs=[in_hbm, in_hbm],
         out_specs=whole_vmem,
@@ -159,7 +160,7 @@
             VMEM((tokens, depth), jnp.bfloat16),
             VMEM((latent, depth), jnp.bfloat16),
             pltpu.SemaphoreType.DMA,
-            pltpu.SemaphoreType.DMA((depth // chunk,)),
+            pltpu.SemaphoreType.DMA((len(spans),)),
         ],
         compiler_params=pltpu.CompilerParams(vmem_limit_bytes=16 * 2**20),
         cost_estimate=pl.CostEstimate(flops=2 * tokens * depth * latent, bytes_accessed=2 * depth * (latent + tokens), transcendentals=0),

time: 14 us -> 15.2 us (1.086)
  the two profiles are of different devices: /device:TPU:0 before, /device:TPU:25 now
where the time goes in v1:
time: 15.2 us; the launch traced here: 15 us
  waiting for transfers between devices  6.31 us (42%)
  Pallas kernels  5.5 us (36%)
  starting transfers between devices  2.48 us (16%)
  between operations  0.68 us (4%)
    ppermute x1, waiting for transfers between devices, run(): here = lax.ppermute(rows, ('pool', 'tp'), pairs)  5.19 us
    pallas_call x1, Pallas kernels, per_device(): pl.pallas_call(functools.partial(project_kernel, spans), out_shape=jax.Sh...  2.99 us
    pallas_call x1, Pallas kernels, attend(): pl.pallas_call(functools.partial(attend_kernel, len(blocks) > 1), out_sha...  1.22 us
    ppermute x1, starting transfers between devices, run(): here = lax.ppermute(rows, ('pool', 'tp'), pairs)  1.05 us
    pallas_call x1, Pallas kernels, mask(): pl.pallas_call(functools.partial(mask_kernel, axes), out_shape=[jax.Shape...  1 us
    ppermute x1, waiting for transfers between devices, run(): return attend(bias, here, lax.ppermute(here, 'tp', [(0, 1), (1, 0)]))  0.91 us
    ppermute x1, starting transfers between devices, per_device(): other = lax.ppermute(partial, 'tp', [(0, 1), (1, 0)])  0.74 us
    ppermute x1, starting transfers between devices, run(): return attend(bias, here, lax.ppermute(here, 'tp', [(0, 1), (1, 0)]))  0.69 us
  transfers between devices with their start and end apart: 3, of which 3 were waited for; matrix products, arithmetic and copies ran while one was open for 0% of the time, Pallas kernels for 8%

profile of v1, /device:TPU:25, one launch (start us, length us, event | category | flops | bytes accessed | tf_op | source)
XLA Modules:
  0.0 15.0 jit_solution(16385655043103989899)
XLA Ops:
  0.0 0.0 copy-start
  0.0 3.0 %project.1.mine_ref = f32[64,576]{1,0:T(8,128)S(1)} custom-call(bf16[64,3584]{1,0:T(8,128)(2,1)} %states_hbm.1, bf16[576,3584]{1,0:T(8,128)(2,1)} %bitcast.5), custom_call_target="tpu_custom_call" | custom-call | flops 264241152 | bytes 4587520 | tf_op jit(solution)/shard_map/project/pallas_call | solution.py:154
  3.0 0.7 %collective-permute-start.7 = (f32[64,576]{1,0:T(8,128)S(1)}, f32[64,576]{1,0:T(8,128)S(1)}, u32[]{:S(2)}, u32[]{:S(2)}) collective-permute-start(f32[64,576]{1,0:T(8,128)S(1)} %project.1.mine_ref), channel_id=1, source_target_pairs={{0,1},{1,0},{2,3},{3,2},{4,5},{5,4},{6,7},{7,6},{8,9},{9,8},{10,11... | collective-permute-start | bytes 442376 | tf_op jit(solution)/shard_map/ppermute | solution.py:178
  3.7 0.1 angles.1
  4.6 0.2 %collective-permute-done.7.other_ref = f32[64,576]{1,0:T(8,128)S(1)} collective-permute-done((f32[64,576]{1,0:T(8,128)S(1)}, f32[64,576]{1,0:T(8,128)S(1)}, u32[]{:S(2)}, u32[]{:S(2)}) %collective-permute-start.7) | collective-permute-done | bytes 147488 | tf_op jit(solution)/shard_map/ppermute | solution.py:178
  4.8 0.0 copy-done
  4.8 0.1 encode.1
  4.9 10.1 %conditional.1 = (bf16[4,64,512]{2,1,0:T(8,128)(2,1)}) conditional(s32[]{:T(128)} %clamp.3, (s32[4]{0:T(128)}, s32[4]{0:T(128)}, bf16[4,64,576]{2,1,0:T(8,128)(2,1)}, bf16[288,128]{1,0:T(8,128)(2,1)S(1)}) %tuple.20, (bf16[288,128]{1,0:T(8,128)(2,1)S(1)}, s32[4]{0:T(128)}, s32[4]{0:T(128)}, ...), branch_computations={%region_0.1_spmd, %region_1.2_spmd, %region_2.3_spmd, %region_3.4_... | conditional | flops 1000 | bytes 594008 | solution.py:240
  4.9 1.0 %collective-permute-start.3 = (bf16[288,128]{1,0:T(8,128)(2,1)S(1)}, bf16[288,128]{1,0:T(8,128)(2,1)S(1)}, u32[]{:S(2)}, u32[]{:S(2)}) collective-permute-start(bf16[288,128]{1,0:T(8,128)(2,1)S(1)} %get-tuple-element.57), channel_id=1, source_target_pairs={{0,8},{1,11},{2,10},{3,9},{4,12},{5,15},{6,14},{7,13},{8,0},{9,3},... | collective-permute-start | bytes 221192 | tf_op jit(solution)/shard_map/cond/branch_2_fun/ppermute | solution.py:233
  6.0 1.0 %mask_and_queries.6 = (f32[1,128]{1,0:T(1,128)S(1)}, bf16[4,64,576]{2,1,0:T(8,128)(2,1)S(1)}) custom-call(s32[4]{0:T(128)} %get-tuple-element.58.owner_hbm, s32[4]{0:T(128)} %get-tuple-element.59.lengths_hbm, bf16[4,64,576]{2,1,0:T(8,128)(2,1)} %get-tuple-element.60.query_hbm), custom_call_target="tpu_custom_call" | custom-call | flops 1000 | bytes 4096 | tf_op jit(solution)/shard_map/cond/branch_2_fun/mask_and_queries/pallas_call | solution.py:189
  7.0 5.2 %collective-permute-done.3.refs_0_ = bf16[288,128]{1,0:T(8,128)(2,1)S(1)} collective-permute-done((bf16[288,128]{1,0:T(8,128)(2,1)S(1)}, bf16[288,128]{1,0:T(8,128)(2,1)S(1)}, u32[]{:S(2)}, u32[]{:S(2)}) %collective-permute-start.3) | collective-permute-done | bytes 73760 | tf_op jit(solution)/shard_map/cond/branch_2_fun/ppermute | solution.py:233
  12.2 0.7 %collective-permute-start.4 = (bf16[288,128]{1,0:T(8,128)(2,1)S(1)}, bf16[288,128]{1,0:T(8,128)(2,1)S(1)}, u32[]{:S(2)}, u32[]{:S(2)}) collective-permute-start(bf16[288,128]{1,0:T(8,128)(2,1)S(1)} %collective-permute-done.3.refs_0_), channel_id=1, source_target_pairs={{0,1},{1,0},{2,3},{3,2},{4,5},{5,4},{6,7},{7,6},{8,9},{9,8},{10,11... | collective-permute-start | bytes 221192 | tf_op jit(solution)/shard_map/cond/branch_2_fun/ppermute | solution.py:235
  12.9 0.9 %collective-permute-done.4.refs_1_ = bf16[288,128]{1,0:T(8,128)(2,1)S(1)} collective-permute-done((bf16[288,128]{1,0:T(8,128)(2,1)S(1)}, bf16[288,128]{1,0:T(8,128)(2,1)S(1)}, u32[]{:S(2)}, u32[]{:S(2)}) %collective-permute-start.4) | collective-permute-done | bytes 73760 | tf_op jit(solution)/shard_map/cond/branch_2_fun/ppermute | solution.py:235
  13.8 1.2 %attend.6 = bf16[4,64,512]{2,1,0:T(8,128)(2,1)} custom-call(bf16[4,64,576]{2,1,0:T(8,128)(2,1)S(1)} %get-tuple-element.63.query_ref, f32[1,128]{1,0:T(1,128)S(1)} %get-tuple-element.64.bias_ref, bf16[288,128]{1,0:T(8,128)(2,1)S(1)} %collective-permute-done.3.refs_0_, bf16[288,128]{1,0:T(8,128)(2,1)S(1)} %collective-permute-done.4.refs_1_), custom_call_target="tpu_custom_call" | custom-call | tf_op jit(solution)/shard_map/cond/branch_2_fun/attend/pallas_call | solution.py:210
Async XLA Ops:
  0.0 4.8 %copy-start = (f32[512]{0:T(512)S(1)}, f32[512]{0:T(512)}, u32[]{:S(2)}) copy-start(f32[512]{0:T(512)} %param.12) | copy-start | bytes 6148
  3.0 1.8 %collective-permute-start.7 = (f32[64,576]{1,0:T(8,128)S(1)}, f32[64,576]{1,0:T(8,128)S(1)}, u32[]{:S(2)}, u32[]{:S(2)}) collective-permute-start(f32[64,576]{1,0:T(8,128)S(1)} %project.1.mine_ref), channel_id=1, source_target_pairs={{0,1},{1,0},{2,3},{3,2},{4,5},{5,4},{6,7},{7,6},{8,9},{9,8},{10,11... | collective-permute-start | bytes 442376 | tf_op jit(solution)/shard_map/ppermute | solution.py:178
  4.9 7.2 %collective-permute-start.3 = (bf16[288,128]{1,0:T(8,128)(2,1)S(1)}, bf16[288,128]{1,0:T(8,128)(2,1)S(1)}, u32[]{:S(2)}, u32[]{:S(2)}) collective-permute-start(bf16[288,128]{1,0:T(8,128)(2,1)S(1)} %get-tuple-element.57), channel_id=1, source_target_pairs={{0,8},{1,11},{2,10},{3,9},{4,12},{5,15},{6,14},{7,13},{8,0},{9,3},... | collective-permute-start | bytes 221192 | tf_op jit(solution)/shard_map/cond/branch_2_fun/ppermute | solution.py:233
  12.2 1.6 %collective-permute-start.4 = (bf16[288,128]{1,0:T(8,128)(2,1)S(1)}, bf16[288,128]{1,0:T(8,128)(2,1)S(1)}, u32[]{:S(2)}, u32[]{:S(2)}) collective-permute-start(bf16[288,128]{1,0:T(8,128)(2,1)S(1)} %collective-permute-done.3.refs_0_), channel_id=1, source_target_pairs={{0,1},{1,0},{2,3},{3,2},{4,5},{5,4},{6,7},{7,6},{8,9},{9,8},{10,11... | collective-permute-start | bytes 221192 | tf_op jit(solution)/shard_map/cond/branch_2_fun/ppermute | solution.py:235
